TPU v7x, 32 devices: a whole 2x2x4 slice. The times are simulated.
32 devices in a mesh: row: 4 (over x, core), col: 8 (over z, y).
Axes of the slice: x: 2, y: 2, z: 4, core: 2. Of those that a mesh axis runs over, the one named last changes fastest.
Arguments:
- vectors: bfloat16 [16, 49152], P(None, ('row', 'col')), may hold values from -6 to 6
- tiles: bfloat16 [4096, 128, 128], P(('row', 'col')), may hold values from -0.046875 to 0.046875
- tile_rows: int32 [4096], P(('row', 'col')), may hold values from 0 to 95
- tile_cols: int32 [4096], P(('row', 'col')), may hold values from 0 to 95
- tile_count: int32 [32], P(('row', 'col')), may hold values from 32 to 128, as said below
Outputs:
- applied: float32 [16, 49152], P(None, ('row', 'col'))
Inputs may be any that keep to these rules, and one draw needn't show every extreme that they name: `tile_count`: each device has between 32 and 128 live slots; some device fills all 128.
All inputs are finite; a program needn't handle non-finite values.
Results may differ from a plain program's by a relative error of at most 0.0003.
Values may be sent and summed in bfloat16 or wider, within the bound.
A program may use at most 64 MiB of HBM per device.

v0:
```python
import jax
import jax.numpy as jnp
from jax import lax
from jax.sharding import PartitionSpec as P


def spread(value, axis, source):
    kept = jnp.where(lax.axis_index(axis) == source, value, 0).astype(value.dtype)
    return lax.psum(kept, axis)


def shards(vectors, tiles, tile_rows, tile_cols, tile_count):
    row_count = lax.axis_size("row")
    col_count = lax.axis_size("col")
    row_index = lax.axis_index("row")
    col_index = lax.axis_index("col")
    mirror_index = col_index % row_count
    vec_count = vectors.shape[0]
    tile_width = tiles.shape[1]
    slot_count = tiles.shape[0]
    own_vectors = lax.all_gather(vectors, "col", axis=1, tiled=True)
    seg_tiles = own_vectors.shape[1] // tile_width
    live_slots = jnp.arange(slot_count, dtype=jnp.int32) < tile_count[0]
    mirrored = live_slots & ((row_index != mirror_index) | (tile_rows != tile_cols))

    def split_blocks(segment):
        return jnp.transpose(segment.reshape(vec_count, seg_tiles, tile_width), (1, 0, 2))

    def merge_back(summed):
        return jnp.transpose(summed, (1, 0, 2)).reshape(vec_count, seg_tiles * tile_width)

    other_vectors = spread(own_vectors, "row", mirror_index)
    picked = jnp.take(split_blocks(other_vectors), tile_cols, axis=0)
    products = jnp.einsum("kvj,kij->kvi", picked, tiles, preferred_element_type=jnp.float32)
    products = jnp.where(live_slots[:, None, None], products, 0.0)
    summed = jax.ops.segment_sum(products, tile_rows, num_segments=seg_tiles)
    plain_sum = merge_back(summed)
    picked = jnp.take(split_blocks(own_vectors), tile_rows, axis=0)
    products = jnp.einsum("kvi,kij->kvj", picked, tiles, preferred_element_type=jnp.float32)
    products = jnp.where(mirrored[:, None, None], products, 0.0)
    summed = jax.ops.segment_sum(products, tile_cols, num_segments=seg_tiles)
    local_sums = merge_back(summed)
    pieces = local_sums.reshape(vec_count, col_count, -1)
    arrived = lax.all_to_all(pieces, "col", split_axis=1, concat_axis=1, tiled=True)
    grouped = jnp.sum(arrived.reshape(vec_count, col_count // row_count, row_count, -1), axis=1)
    share = lax.psum_scatter(grouped, "row", scatter_dimension=1, tiled=True)
    mirror_sum = share.reshape(vec_count, -1)
    applied = lax.psum_scatter(plain_sum, "col", scatter_dimension=1, tiled=True) + mirror_sum
    return applied


def solution(mesh):
    return jax.shard_map(
        shards,
        mesh=mesh,
        in_specs=(
            P(None, ("row", "col")),
            P(("row", "col"), None, None),
            P(("row", "col")),
            P(("row", "col")),
            P(("row", "col")),
        ),
        out_specs=P(None, ("row", "col")),
        check_vma=False,
    )
```

profile of v0, /device:TPU:0, one launch (start us, length us, event | category | flops | bytes accessed | tf_op | source)
XLA Modules:
  0.0 182.0 jit_solution(15316486115447258305)
XLA Ops:
  6.5 0.0 all-reduce.2.cloned.1.call-start
  6.5 32.9 %all_gather.3 = bf16[16,12288]{1,0:T(8,128)(2,1)S(1)} all-gather(bf16[16,1536]{1,0:T(8,128)(2,1)} %param.7), channel_id=1, replica_groups=mesh['row'=4,'col'=8] {'col'}, dimensions={1}, use_global_device_ids=true | all-gather | bytes 442368 | tf_op jit(solution)/shard_map/all_gather | solution.py:21
  39.5 0.8 bitcast_bitcast_fusion.1
  40.3 0.0 all-reduce.2.cloned.1.call-update
  40.3 0.0 reduce-scatter.3.cloned.1.call-start
  40.4 0.1 bitcast_bitcast_fusion
  40.5 0.7 compare_select_fusion.1
  41.8 0.7 compare_select_fusion
  42.5 0.0 copy-start
  42.5 0.7 gather_fusion.1
  43.2 0.7 or_and_fusion
  43.9 30.3 %all-reduce.2.cloned.1.call-done = bf16[96,16,128]{2,1,0:T(8,128)(2,1)} async-done(((bf16[96,16,128]{2,1,0:T(8,128)(2,1)}), bf16[96,16,128]{2,1,0:T(8,128)(2,1)}) %all-reduce.2.cloned.1.call-update) | async-done | bytes 393232 | tf_op jit(solution)/shard_map/psum | solution.py:9
  74.2 1.7 gather_fusion
  75.9 4.5 %convolution_select_fusion.1 = f32[128,16,128]{2,1,0:T(8,128)S(1)} fusion(bf16[128,128,128]{2,1,0:T(8,128)(2,1)} %param.8, bf16[128,16,128]{2,1,0:T(8,128)(2,1)S(1)} %gather_fusion, pred[128]{0:T(512)(128)(4,1)S(1)} %get-tuple-element.7, pred[128]{0:T(512)(128)(4,1)S(1)} %iota_compare_fusion), kind=kOutput, calls=%fused_computation.5 | convolution fusion | flops 67633152 | bytes 5767424 | tf_op jit(solution)/shard_map/kvj,kij->kvi/dot_general | solution.py:34
  80.4 0.1 broadcast.12.clone
  80.4 0.0 copy-done
  80.4 5.2 %scatter_fusion = f32[96,16,128]{2,1,0:T(8,128)S(1)} fusion(f32[96,16,128]{2,1,0:T(8,128)S(1)} %broadcast.12.clone, s32[128]{0:T(128)S(1)} %copy-done, f32[128,16,128]{2,1,0:T(8,128)S(1)} %convolution_select_fusion.1), kind=kCustom, calls=%fused_computation.2 | custom fusion | flops 262144 | bytes 3146240 | tf_op jit(solution)/shard_map/scatter-add | solution.py:36
  85.7 0.0 copy-start.1
  85.7 0.9 copy_bitcast_fusion
  86.6 0.0 reduce-scatter.3.cloned.1.call-update
  86.6 0.0 reduce-scatter.5.cloned.1.call-start
  86.7 3.4 %convolution_select_fusion = f32[128,16,128]{2,1,0:T(8,128)S(1)} fusion(bf16[128,128,128]{2,1,0:T(8,128)(2,1)} %param.8, bf16[128,16,128]{2,1,0:T(8,128)(2,1)S(1)} %gather_fusion.1, pred[128]{0:T(512)(128)(4,1)S(1)} %get-tuple-element.8, pred[128]{0:T(512)(128)(4,1)S(1)} %get-tuple-element.6), kind=kOutput, calls=%fused_computation.4 | convolution fusion | flops 67633152 | bytes 5767424 | tf_op jit(solution)/shard_map/kvi,kij->kvj/dot_general | solution.py:39
  90.1 0.1 broadcast.12.clone.1
  90.2 0.0 copy-done.1
  90.2 5.2 %scatter_fusion.1 = f32[96,16,128]{2,1,0:T(8,128)S(1)} fusion(f32[96,16,128]{2,1,0:T(8,128)S(1)} %broadcast.12.clone.1, s32[128]{0:T(128)S(1)} %copy-done.1, f32[128,16,128]{2,1,0:T(8,128)S(1)} %convolution_select_fusion), kind=kCustom, calls=%fused_computation.3 | custom fusion | flops 262144 | bytes 3146240 | tf_op jit(solution)/shard_map/scatter-add | solution.py:41
  95.4 0.3 copy.19
  95.6 0.1 reshape_reshape.3
  95.8 0.5 copy.20
  96.2 28.2 %all_to_all.5 = f32[16,8,1536]{2,0,1:T(8,128)S(1)} all-to-all(f32[16,8,1536]{2,0,1:T(8,128)S(1)} %copy.20), channel_id=1, replica_groups=mesh['row'=4,'col'=8] {'col'}, dimensions={1} | all-to-all | bytes 1572864 | tf_op jit(solution)/shard_map/all_to_all | solution.py:44
  124.4 0.8 reduce_sum.9
  125.2 0.0 reduce-scatter.5.cloned.1.call-update
  125.3 26.2 %reduce-scatter.3.cloned.1.call-done = f32[16,1536]{1,0:T(8,128)} async-done(((f32[16,12288]{1,0:T(8,128)}), f32[16,1536]{1,0:T(8,128)}) %reduce-scatter.3.cloned.1.call-update) | async-done | bytes 98320 | tf_op jit(solution)/shard_map/reduce_scatter | solution.py:48
  151.5 22.3 %reduce-scatter.5.cloned.1.call-done = f32[16,1,1536]{2,0,1:T(8,128)} async-done(((f32[16,4,1536]{2,0,1:T(8,128)}), f32[16,1,1536]{2,0,1:T(8,128)}) %reduce-scatter.5.cloned.1.call-update) | async-done | bytes 98320 | tf_op jit(solution)/shard_map/reduce_scatter | solution.py:46
  173.8 1.6 bitcast_add_fusion
  (3 shorter events, 0.0 us)
Async XLA Ops:
  6.5 67.6 %all-reduce.2.cloned.1.call-start = ((), (), s32[]{:S(2)}) async-start(), calls=%async_computation.3 | async-start | bytes 786432 | tf_op jit(solution)/shard_map/psum | solution.py:9
  40.3 111.2 %reduce-scatter.3.cloned.1.call-start = ((), (), s32[]{:S(2)}) async-start(), calls=%async_computation.4 | async-start | bytes 884736 | tf_op jit(solution)/shard_map/reduce_scatter | solution.py:48
  42.5 38.0 %copy-start = (s32[128]{0:T(128)S(1)}, s32[128]{0:T(128)}, u32[]{:S(2)}) copy-start(s32[128]{0:T(128)} %param.9) | copy-start | bytes 1540
  85.7 4.5 %copy-start.1 = (s32[128]{0:T(128)S(1)}, s32[128]{0:T(128)}, u32[]{:S(2)}) copy-start(s32[128]{0:T(128)} %param.10) | copy-start | bytes 1540
  86.6 87.2 %reduce-scatter.5.cloned.1.call-start = ((), (), s32[]{:S(2)}) async-start(), calls=%async_computation.5 | async-start | bytes 491520 | tf_op jit(solution)/shard_map/reduce_scatter | solution.py:46
Sparse Core Ops, SparseCore 0:
  40.5 33.6 all-reduce.1
  86.7 64.7 reduce-scatter.2
  154.0 19.7 reduce-scatter.4
where the time goes:
time: 182 us
  waiting for transfers between devices  78.9 us (43%)
  blocking collectives  61.2 us (34%)
  other arithmetic  15.6 us (9%)
  between operations  13.9 us (8%)
  matrix products  7.96 us (4%)
  local copies, waits for them, and re-layouts  4.37 us (2%)
    all_gather x1, blocking collectives, shards(): own_vectors = lax.all_gather(vectors, 'col', axis=1, tiled=True)  32.9 us
    psum x1, waiting for transfers between devices, spread(): return lax.psum(kept, axis)  30.3 us
    all_to_all x1, blocking collectives, shards(): lax.all_to_all(pieces, 'col', split_axis=1, concat_axis=1, tiled=True)  28.2 us
    reduce_scatter x1, waiting for transfers between devices, shards(): lax.psum_scatter(plain_sum, 'col', scatter_dimension=1, tiled=True)  26.2 us
    reduce_scatter x1, waiting for transfers between devices, shards(): share = lax.psum_scatter(grouped, 'row', scatter_dimension=1, tiled=True)  22.3 us
    scatter-add x1, other arithmetic, shards(): summed = jax.ops.segment_sum(products, tile_rows, num_segments=seg_tiles)  5.2 us
    scatter-add x1, other arithmetic, shards(): summed = jax.ops.segment_sum(products, tile_cols, num_segments=seg_tiles)  5.18 us
    dot_general x1, matrix products, shards(): jnp.einsum('kvj,kij->kvi', picked, tiles, preferred_element_type=jnp.floa...  4.51 us
  transfers between devices with their start and end apart: 3, of which 3 were waited for; matrix products, arithmetic and copies ran while one was open for 7% of the time, Pallas kernels for 0%

commit v1 on v0

v1 whole, which is shorter than its diff:
```python
import functools

import jax
import jax.numpy as jnp
from jax import lax
from jax.experimental import pallas as pl
from jax.experimental.pallas import tpu as pltpu
from jax.sharding import PartitionSpec as P

MESH = pl.DeviceIdType.MESH
VMEM_BYTES = 48 * 1024 * 1024


def remote(src, dst, send_sem, recv_sem, row, col):
    return pltpu.make_async_remote_copy(
        src_ref=src,
        dst_ref=dst,
        send_sem=send_sem,
        recv_sem=recv_sem,
        device_id=(row, col),
        device_id_type=MESH,
    )


def greet(row, col):
    pl.semaphore_signal(
        pltpu.get_barrier_semaphore(), inc=1, device_id=(row, col), device_id_type=MESH
    )


def order_table(lines, key, operand, places):
    slots = key.shape[1]
    keys = jnp.broadcast_to(key, (slots, slots))
    down = keys.T
    at = lax.broadcasted_iota(jnp.int32, (slots, slots), 0)
    along = lax.broadcasted_iota(jnp.int32, (slots, slots), 1)
    ahead = (down < keys) | ((down == keys) & (at < along))
    rank = jnp.sum(ahead.astype(jnp.int32), axis=0, keepdims=True)
    hit = jnp.broadcast_to(rank, (slots, slots)).T == along
    operands = jnp.broadcast_to(operand, (slots, slots)).T

    def pick(values):
        return jnp.sum(jnp.where(hit, values, 0), axis=0, keepdims=True)

    lines[0] = pick(at)
    lines[1] = pick(operands)
    lines[2] = pick(down)
    place = lax.broadcasted_iota(jnp.int32, (slots, slots), 1)
    for n in range(places // slots):
        spot = place + n * slots
        upto = jnp.sum((down <= spot).astype(jnp.int32), axis=0, keepdims=True)
        before = jnp.sum((down < spot).astype(jnp.int32), axis=0, keepdims=True)
        lines[3 + n] = jnp.where(upto > before, upto - 1, slots)


def kernel(
    rows, cols, width, group,
    x_hbm, tiles_hbm, rows_ref, cols_ref, count_ref, out,
    x_in, tiles, own, mir, lines, table, run_p, run_m, stage_p, stage_m,
    y_in, y_sum, z_in, a_in, a_sum, b_in, b_sum, m_in,
    local, line_send, mate_send, own_recv, mir_send, mir_recv,
    y_send, y_recv, z_send, z_recv, a_send, a_recv, b_send, b_recv, m_send, m_recv,
):
    r, c = lax.axis_index("row"), lax.axis_index("col")
    half, row_half = cols // 2, rows // 2
    hi, lo = c // 2, c % 2
    mate = c + 1 - 2 * lo
    row_lo, row_hi = r % 2, r // 2
    row_mate = r + 1 - 2 * row_lo
    share = cols // rows
    target = c % rows
    turn = c // rows
    size = y_in.shape[1]
    slots = tiles.shape[0]
    owns = target == r
    own_piece = (c // share == r) & owns

    def is_self(j):
        return owns & (share * r + j == c)

    x_copy = pltpu.make_async_copy(x_hbm, x_in, local.at[0])
    tiles_copy = pltpu.make_async_copy(tiles_hbm, tiles, local.at[1])
    x_copy.start()
    tiles_copy.start()

    greet(r, mate)
    for d in range(1, half):
        greet(r, lax.rem(hi + half - d, half) * 2 + lo)
    greet(row_mate, c)
    for d in range(1, row_half):
        greet(lax.rem(row_hi + row_half - d, row_half) * 2 + row_lo, c)
    for i in range(share):
        @pl.when(jnp.logical_not((c // share == r) & (r + rows * i == c)))
        def _(i=i):
            greet(c // share, r + rows * i)

    @pl.when(jnp.logical_not(owns))
    def _():
        greet(target, c)

    x_copy.wait()
    for t in range(size):
        own[c * size + t] = x_in[:, t * width:(t + 1) * width]
    receivers = half + row_half + share - jnp.where(own_piece, 1, 0) + jnp.where(owns, rows - 1, 0)
    pl.semaphore_wait(pltpu.get_barrier_semaphore(), receivers)

    def part(ref, index, count=1):
        return ref.at[pl.ds(index * size, count * size)]

    def to_line(d):
        there = lax.rem(hi + d, half) * 2 + lo
        return remote(part(own, c), part(own, c), line_send.at[d - 1], own_recv.at[c], r, there)

    def to_mate(index, n):
        return remote(part(own, index), part(own, index), mate_send.at[n], own_recv.at[index], r, mate)

    def mirror_sends(index, n):
        return [
            remote(
                part(own, index), part(mir, index), mir_send.at[n, d - 1], mir_recv.at[index],
                lax.rem(r + d, rows), c,
            )
            for d in range(1, rows)
        ]

    order = [c]
    for d in range(1, half):
        order.append(lax.rem(hi + half - d, half) * 2 + lo)
    order.append(mate)
    for d in range(1, half):
        order.append(lax.rem(hi + half - d, half) * 2 + 1 - lo)

    for d in range(1, half):
        to_line(d).start()
    to_mate(c, 0).start()

    @pl.when(owns)
    def _():
        for copy in mirror_sends(c, 0):
            copy.start()

    count = count_ref[0]
    live = lax.broadcasted_iota(jnp.int32, (1, slots), 1) < count
    row_line, col_line = rows_ref[...], cols_ref[...]
    never = own.shape[0]
    places = (lines.shape[0] // 2 - 3) * slots
    lines_m, lines_p = lines.at[0:lines.shape[0] // 2], lines.at[lines.shape[0] // 2:lines.shape[0]]
    both = live & (jnp.logical_not(owns) | (row_line != col_line))
    order_table(lines_m, jnp.where(both, col_line, never), row_line, places)
    order_table(lines_p, jnp.where(live, row_line, never), col_line, places)
    table_copy = pltpu.make_async_copy(lines, table, local.at[2])
    table_copy.start()
    run_p[slots] = jnp.zeros_like(run_p[slots])
    run_m[slots] = jnp.zeros_like(run_m[slots])

    for n in range(cols):
        index = order[n]
        if n:
            to_mate(index, 0).wait_recv()

            if n < half:
                to_mate(index, n).start()

        @pl.when(owns)
        def _(index=index, n=n):
            if n:
                for copy in mirror_sends(index, n):
                    copy.start()
            for t in range(size):
                mir[index * size + t] = own[index * size + t]

    table_copy.wait()
    tiles_copy.wait()

    def products(base, source, runs, contract):
        def body(g, carry):
            run, before = carry
            found = []
            for u in range(group):
                p = g * group + u
                slot = table[base, 0, p]
                found.append(
                    lax.dot_general(
                        source[table[base + 1, 0, p]], tiles[slot], (((1,), (contract,)), ((), ())),
                        preferred_element_type=jnp.float32,
                    )
                )
            for u in range(group):
                p = g * group + u
                key = table[base + 2, 0, p]
                run = jnp.where(key == before, run, 0.0) + found[u]
                runs[p] = run
                before = key
            return run, before

        start = (jnp.zeros((own.shape[1], width), jnp.float32), jnp.int32(-1))
        lax.fori_loop(0, slots // group, body, start)

    base_p = lines.shape[0] // 2

    def sum_at(base, runs, place):
        return runs[table[base + 3 + place // slots, 0, place % slots]]

    def mirror_at(place):
        return sum_at(0, run_m, place)

    def plain_at(place):
        return sum_at(base_p, run_p, place)

    def a_copy(d):
        return remote(stage_m.at[d], a_in.at[d], a_send.at[d], a_recv.at[d], row_mate, c)

    def b_copy(d):
        there = lax.rem(row_hi + d, row_half) * 2 + row_lo
        return remote(a_sum.at[d], b_in.at[d - 1], b_send.at[d - 1], b_recv.at[d - 1], there, c)

    def y_copy(d):
        return remote(stage_p.at[d], y_in.at[d], y_send.at[d], y_recv.at[d], r, mate)

    def z_copy(d):
        there = lax.rem(hi + d, half) * 2 + lo
        return remote(y_sum.at[d], z_in.at[d - 1], z_send.at[d - 1], z_recv.at[d - 1], r, there)

    def m_copy(j):
        return remote(
            part(b_sum, j), m_in.at[turn], m_send.at[j], m_recv.at[turn], target, share * r + j
        )

    row_turns = list(range(1, row_half)) + [0]
    turns = list(range(1, half)) + [0]

    products(0, own, run_m, 0)
    for d in row_turns:
        first = (2 * lax.rem(row_hi + d, row_half) + 1 - row_lo) * share * size
        for t in range(share * size):
            stage_m[d, t] = mirror_at(first + t)
        a_copy(d).start()

    @pl.when(jnp.logical_not(owns))
    def _():
        for n in range(cols):
            remote(
                part(own, order[n]), part(mir, order[n]), mir_send.at[n, 0], mir_recv.at[order[n]], row_mate, c
            ).wait_recv()

    products(base_p, mir, run_p, 1)
    for d in turns:
        first = (2 * lax.rem(hi + d, half) + 1 - lo) * size
        for t in range(size):
            stage_p[d, t] = plain_at(first + t)
        y_copy(d).start()
    for d in row_turns:
        a_copy(d).wait_recv()
        first = (2 * lax.rem(row_hi + d, row_half) + row_lo) * share * size
        for t in range(share * size):
            a_sum[d, t] = mirror_at(first + t) + a_in[d, t]
        if d:
            b_copy(d).start()
    for d in turns[:-1]:
        y_copy(d).wait_recv()
        first = (2 * lax.rem(hi + d, half) + lo) * size
        for t in range(size):
            y_sum[d, t] = plain_at(first + t) + y_in[d, t]
        z_copy(d).start()
    for d in range(1, row_half):
        b_copy(d).wait_recv()
    total = a_sum[0]
    for d in range(1, row_half):
        total = total + b_in[d - 1]
    b_sum[...] = total
    for j in range(share):
        @pl.when(jnp.logical_not(is_self(j)))
        def _(j=j):
            m_copy(j).start()

        @pl.when(is_self(j))
        def _(j=j):
            m_in[turn] = b_sum[j * size:(j + 1) * size]
    y_copy(0).wait_recv()
    for t in range(size):
        y_sum[0, t] = plain_at((2 * hi + lo) * size + t) + y_in[0, t]
    for d in range(1, half):
        z_copy(d).wait_recv()
        y_sum[0] += z_in[d - 1]
    for i in range(share):
        @pl.when(jnp.logical_not((c // share == r) & (r + rows * i == c)))
        def _(i=i):
            remote(
                part(b_sum, 0), m_in.at[i], m_send.at[0], m_recv.at[i], r, mate
            ).wait_recv()
    for t in range(size):
        value = y_sum[0, t]
        for i in range(share):
            value = value + m_in[i, t]
        out[:, t * width:(t + 1) * width] = value

    for d in range(1, half):
        to_line(d).wait_send()
    for n in range(half):
        to_mate(order[n], n).wait_send()

    @pl.when(owns)
    def _():
        for n in range(cols):
            for copy in mirror_sends(order[n], n):
                copy.wait_send()

    for d in row_turns:
        a_copy(d).wait_send()
    for d in turns:
        y_copy(d).wait_send()
    for d in range(1, row_half):
        b_copy(d).wait_send()
    for d in range(1, half):
        z_copy(d).wait_send()
    for j in range(share):
        @pl.when(jnp.logical_not(is_self(j)))
        def _(j=j):
            m_copy(j).wait_send()


def shards(vectors, tiles, tile_rows, tile_cols, tile_count):
    rows, cols = lax.axis_size("row"), lax.axis_size("col")
    slots, width = tiles.shape[0], tiles.shape[1]
    vec_count, length = vectors.shape
    size = length // width
    share = cols // rows
    half, row_half = cols // 2, rows // 2
    places = -(-(cols * size) // slots)
    dma = pltpu.SemaphoreType.DMA

    def room(*lead):
        return pltpu.VMEM((*lead, vec_count, width), jnp.float32)

    segment = pltpu.VMEM((cols * size, vec_count, width), vectors.dtype)
    on_vmem = pl.BlockSpec(memory_space=pltpu.VMEM)
    return pl.pallas_call(
        functools.partial(kernel, rows, cols, width, 8 if slots % 8 == 0 else 1),
        out_shape=jax.ShapeDtypeStruct((vec_count, length), jnp.float32),
        in_specs=[
            pl.BlockSpec(memory_space=pl.ANY),
            pl.BlockSpec(memory_space=pl.ANY),
            on_vmem,
            on_vmem,
            pl.BlockSpec(memory_space=pltpu.SMEM),
        ],
        out_specs=on_vmem,
        scratch_shapes=[
            pltpu.VMEM((vec_count, length), vectors.dtype),
            pltpu.VMEM(tiles.shape, tiles.dtype),
            segment,
            segment,
            pltpu.VMEM((2 * (3 + places), 1, slots), jnp.int32),
            pltpu.SMEM((2 * (3 + places), 1, slots), jnp.int32),
            room(slots + 1),
            room(slots + 1),
            room(half, size),
            room(row_half, share * size),
            room(half, size),
            room(half, size),
            room(half, size),
            room(row_half, share * size),
            room(row_half, share * size),
            room(row_half, share * size),
            room(share * size),
            room(share, size),
            dma((3,)), dma((half,)), dma((half,)), dma((cols,)), dma((cols, rows)), dma((cols,)),
            dma((half,)), dma((half,)), dma((half,)), dma((half,)),
            dma((row_half,)), dma((row_half,)), dma((row_half,)), dma((row_half,)),
            dma((share,)), dma((share,)),
        ],
        compiler_params=pltpu.CompilerParams(
            collective_id=0, has_side_effects=True, vmem_limit_bytes=VMEM_BYTES
        ),
        name="apply_symmetric",
    )(vectors, tiles, tile_rows.reshape(1, slots), tile_cols.reshape(1, slots), tile_count)


def solution(mesh):
    return jax.shard_map(
        shards,
        mesh=mesh,
        in_specs=(
            P(None, ("row", "col")),
            P(("row", "col"), None, None),
            P(("row", "col")),
            P(("row", "col")),
            P(("row", "col")),
        ),
        out_specs=P(None, ("row", "col")),
        check_vma=False,
    )
```

time: 182 us -> 50.8 us (0.28)
  waiting for transfers between devices: 78.9 us -> 0 us
  blocking collectives: 61.2 us -> 0 us
  Pallas kernels: 0 us -> 44.2 us
  other arithmetic: 15.6 us -> 0 us
  between operations: 13.9 us -> 0.67 us
  matrix products: 7.96 us -> 0 us
    reduce_scatter x2 -> x0, waiting for transfers between devices: 48.6 us -> none  [the longest x1 26.2 us: shards(): lax.psum_scatter(plain_sum, 'col', scatter_dimension=1, tiled=True)]
    pallas_call x0 -> x1, Pallas kernels: none -> 44.2 us  [shards(): pl.pallas_call(functools.partial(kernel, rows, cols, width, 8 if slots %...]
    all_gather x1 -> x0, blocking collectives: 32.9 us -> none  [shards(): own_vectors = lax.all_gather(vectors, 'col', axis=1, tiled=True)]
    psum x1 -> x0, waiting for transfers between devices: 30.3 us -> none  [spread(): return lax.psum(kept, axis)]
    all_to_all x1 -> x0, blocking collectives: 28.2 us -> none  [shards(): lax.all_to_all(pieces, 'col', split_axis=1, concat_axis=1, tiled=True)]
    scatter-add x2 -> x0, other arithmetic: 10.4 us -> none  [the longest x1 5.2 us: shards(): summed = jax.ops.segment_sum(products, tile_rows, num_segments=seg_tiles)]
    dot_general x2 -> x0, matrix products: 7.96 us -> none  [the longest x1 4.51 us: shards(): jnp.einsum('kvj,kij->kvi', picked, tiles, preferred_element_type=jnp.floa...]
    unnamed x4 -> x9, local copies, waits for them, and re-layouts: 0.01 us -> 4.93 us
  transfers between devices with their start and end apart: 3 -> 0, of which waited for: 3 -> 0; matrix products, arithmetic and copies ran while one was open for 7% -> 0% of each run, Pallas kernels for 0% -> 0%
where the time goes in v1:
time: 50.8 us; the launch traced here: 49.8 us
  Pallas kernels  44.2 us (87%)
  local copies, waits for them, and re-layouts  4.93 us (10%)
  between operations  0.67 us (1%)
    pallas_call x1, Pallas kernels, shards(): pl.pallas_call(functools.partial(kernel, rows, cols, width, 8 if slots %...  44.2 us
    unnamed x9, local copies, waits for them, and re-layouts  4.93 us

profile of v1, /device:TPU:0, one launch (start us, length us, event | category | flops | bytes accessed | tf_op | source)
XLA Modules:
  0.0 49.8 jit_solution(9044221514370313174)
XLA Ops:
  0.7 0.0 copy-start
  0.7 2.2 %copy-done = bf16[128,128,128]{2,1,0:T(8,128)(2,1)S(1)} copy-done((bf16[128,128,128]{2,1,0:T(8,128)(2,1)S(1)}, bf16[128,128,128]{2,1,0:T(8,128)(2,1)}, u32[]{:S(2)}) %copy-start) | copy-done | bytes 4194328
  2.8 0.0 copy-start.1
  2.8 0.8 %copy-done.1 = bf16[16,1536]{1,0:T(8,128)(2,1)S(1)} copy-done((bf16[16,1536]{1,0:T(8,128)(2,1)S(1)}, bf16[16,1536]{1,0:T(8,128)(2,1)}, u32[]{:S(2)}) %copy-start.1) | copy-done | bytes 49176
  3.6 0.0 copy-start.2
  3.6 0.7 %copy-done.2 = s32[128]{0:T(128)S(1)} copy-done((s32[128]{0:T(128)S(1)}, s32[128]{0:T(128)}, u32[]{:S(2)}) %copy-start.2) | copy-done | bytes 536
  4.3 0.0 copy-start.3
  4.3 0.7 %copy-done.3 = s32[128]{0:T(128)S(1)} copy-done((s32[128]{0:T(128)S(1)}, s32[128]{0:T(128)}, u32[]{:S(2)}) %copy-start.3) | copy-done | bytes 536
  5.0 44.2 %apply_symmetric.1 = f32[16,1536]{1,0:T(8,128)S(1)} custom-call(bf16[16,1536]{1,0:T(8,128)(2,1)S(1)} %copy-done.1, bf16[128,128,128]{2,1,0:T(8,128)(2,1)S(1)} %copy-done, s32[1,128]{1,0:T(1,128)S(1)} %bitcast.2, s32[1,128]{1,0:T(1,128)S(1)} %bitcast.3, s32[1]{0:T(128)S(6)} %copy.7.count_ref), custom_call_target="tpu_custom_call" | custom-call | tf_op jit(solution)/shard_map/apply_symmetric/pallas_call | solution.py:337
  49.1 0.6 %copy.8 = f32[16,1536]{1,0:T(8,128)} copy(f32[16,1536]{1,0:T(8,128)S(1)} %apply_symmetric.1) | data formatting | bytes 196608
Async XLA Ops:
  0.7 2.2 %copy-start = (bf16[128,128,128]{2,1,0:T(8,128)(2,1)S(1)}, bf16[128,128,128]{2,1,0:T(8,128)(2,1)}, u32[]{:S(2)}) copy-start(bf16[128,128,128]{2,1,0:T(8,128)(2,1)} %tiles_hbm.1) | copy-start | bytes 12582916
  2.8 0.8 %copy-start.1 = (bf16[16,1536]{1,0:T(8,128)(2,1)S(1)}, bf16[16,1536]{1,0:T(8,128)(2,1)}, u32[]{:S(2)}) copy-start(bf16[16,1536]{1,0:T(8,128)(2,1)} %x_hbm.1) | copy-start | bytes 147460
  3.6 0.7 %copy-start.2 = (s32[128]{0:T(128)S(1)}, s32[128]{0:T(128)}, u32[]{:S(2)}) copy-start(s32[128]{0:T(128)} %param.7) | copy-start | bytes 1540
  4.3 0.7 %copy-start.3 = (s32[128]{0:T(128)S(1)}, s32[128]{0:T(128)}, u32[]{:S(2)}) copy-start(s32[128]{0:T(128)} %param.8) | copy-start | bytes 1540

commit v2 on v1

--- a/solution.py
+++ b/solution.py
@@ -8,7 +8,7 @@
 from jax.sharding import PartitionSpec as P
 
 MESH = pl.DeviceIdType.MESH
-VMEM_BYTES = 48 * 1024 * 1024
+VMEM_BYTES = 60 * 1024 * 1024
 
 
 def remote(src, dst, send_sem, recv_sem, row, col):
@@ -55,8 +55,8 @@
 
 def kernel(
     rows, cols, width, group,
-    x_hbm, tiles_hbm, rows_ref, cols_ref, count_ref, out,
-    x_in, tiles, own, mir, lines, table, run_p, run_m, stage_p, stage_m,
+    x_hbm, tiles_hbm, rows_hbm, cols_hbm, count_ref, out,
+    x_in, tiles, rows_ref, cols_ref, own, mir, lines_m, lines_p, table_m, table_p, run_p, run_m, stage_p, stage_m,
     y_in, y_sum, z_in, a_in, a_sum, b_in, b_sum, m_in,
     local, line_send, mate_send, own_recv, mir_send, mir_recv,
     y_send, y_recv, z_send, z_recv, a_send, a_recv, b_send, b_recv, m_send, m_recv,
@@ -80,8 +80,11 @@
 
     x_copy = pltpu.make_async_copy(x_hbm, x_in, local.at[0])
     tiles_copy = pltpu.make_async_copy(tiles_hbm, tiles, local.at[1])
+    rows_copy = pltpu.make_async_copy(rows_hbm, rows_ref, local.at[2])
+    cols_copy = pltpu.make_async_copy(cols_hbm, cols_ref, local.at[3])
     x_copy.start()
-    tiles_copy.start()
+    rows_copy.start()
+    cols_copy.start()
 
     greet(r, mate)
     for d in range(1, half):
@@ -101,6 +104,7 @@
     x_copy.wait()
     for t in range(size):
         own[c * size + t] = x_in[:, t * width:(t + 1) * width]
+    tiles_copy.start()
     receivers = half + row_half + share - jnp.where(own_piece, 1, 0) + jnp.where(owns, rows - 1, 0)
     pl.semaphore_wait(pltpu.get_barrier_semaphore(), receivers)
 
@@ -139,17 +143,15 @@
         for copy in mirror_sends(c, 0):
             copy.start()
 
-    count = count_ref[0]
-    live = lax.broadcasted_iota(jnp.int32, (1, slots), 1) < count
-    row_line, col_line = rows_ref[...], cols_ref[...]
+    rows_copy.wait()
+    cols_copy.wait()
+    live = lax.broadcasted_iota(jnp.int32, (1, slots), 1) < count_ref[0]
     never = own.shape[0]
-    places = (lines.shape[0] // 2 - 3) * slots
-    lines_m, lines_p = lines.at[0:lines.shape[0] // 2], lines.at[lines.shape[0] // 2:lines.shape[0]]
-    both = live & (jnp.logical_not(owns) | (row_line != col_line))
-    order_table(lines_m, jnp.where(both, col_line, never), row_line, places)
-    order_table(lines_p, jnp.where(live, row_line, never), col_line, places)
-    table_copy = pltpu.make_async_copy(lines, table, local.at[2])
-    table_copy.start()
+    places = (lines_m.shape[0] - 3) * slots
+    both = live & (jnp.logical_not(owns) | (rows_ref[...] != cols_ref[...]))
+    order_table(lines_m, jnp.where(both, cols_ref[...], never), rows_ref[...], places)
+    table_m_copy = pltpu.make_async_copy(lines_m, table_m, local.at[4])
+    table_m_copy.start()
     run_p[slots] = jnp.zeros_like(run_p[slots])
     run_m[slots] = jnp.zeros_like(run_m[slots])
 
@@ -169,25 +171,25 @@
             for t in range(size):
                 mir[index * size + t] = own[index * size + t]
 
-    table_copy.wait()
+    table_m_copy.wait()
     tiles_copy.wait()
 
-    def products(base, source, runs, contract):
+    def products(table, source, runs, contract):
         def body(g, carry):
             run, before = carry
             found = []
             for u in range(group):
                 p = g * group + u
-                slot = table[base, 0, p]
+                slot = table[0, 0, p]
                 found.append(
                     lax.dot_general(
-                        source[table[base + 1, 0, p]], tiles[slot], (((1,), (contract,)), ((), ())),
+                        source[table[1, 0, p]], tiles[slot], (((1,), (contract,)), ((), ())),
                         preferred_element_type=jnp.float32,
                     )
                 )
             for u in range(group):
                 p = g * group + u
-                key = table[base + 2, 0, p]
+                key = table[2, 0, p]
                 run = jnp.where(key == before, run, 0.0) + found[u]
                 runs[p] = run
                 before = key
@@ -196,16 +198,14 @@
         start = (jnp.zeros((own.shape[1], width), jnp.float32), jnp.int32(-1))
         lax.fori_loop(0, slots // group, body, start)
 
-    base_p = lines.shape[0] // 2
-
-    def sum_at(base, runs, place):
-        return runs[table[base + 3 + place // slots, 0, place % slots]]
+    def sum_at(table, runs, place):
+        return runs[table[3 + place // slots, 0, place % slots]]
 
     def mirror_at(place):
-        return sum_at(0, run_m, place)
+        return sum_at(table_m, run_m, place)
 
     def plain_at(place):
-        return sum_at(base_p, run_p, place)
+        return sum_at(table_p, run_p, place)
 
     def a_copy(d):
         return remote(stage_m.at[d], a_in.at[d], a_send.at[d], a_recv.at[d], row_mate, c)
@@ -229,26 +229,15 @@
     row_turns = list(range(1, row_half)) + [0]
     turns = list(range(1, half)) + [0]
 
-    products(0, own, run_m, 0)
+    products(table_m, own, run_m, 0)
     for d in row_turns:
         first = (2 * lax.rem(row_hi + d, row_half) + 1 - row_lo) * share * size
         for t in range(share * size):
             stage_m[d, t] = mirror_at(first + t)
         a_copy(d).start()
-
-    @pl.when(jnp.logical_not(owns))
-    def _():
-        for n in range(cols):
-            remote(
-                part(own, order[n]), part(mir, order[n]), mir_send.at[n, 0], mir_recv.at[order[n]], row_mate, c
-            ).wait_recv()
-
-    products(base_p, mir, run_p, 1)
-    for d in turns:
-        first = (2 * lax.rem(hi + d, half) + 1 - lo) * size
-        for t in range(size):
-            stage_p[d, t] = plain_at(first + t)
-        y_copy(d).start()
+    order_table(lines_p, jnp.where(live, rows_ref[...], never), cols_ref[...], places)
+    table_p_copy = pltpu.make_async_copy(lines_p, table_p, local.at[5])
+    table_p_copy.start()
     for d in row_turns:
         a_copy(d).wait_recv()
         first = (2 * lax.rem(row_hi + d, row_half) + row_lo) * share * size
@@ -256,12 +245,21 @@
             a_sum[d, t] = mirror_at(first + t) + a_in[d, t]
         if d:
             b_copy(d).start()
-    for d in turns[:-1]:
-        y_copy(d).wait_recv()
-        first = (2 * lax.rem(hi + d, half) + lo) * size
+    table_p_copy.wait()
+
+    @pl.when(jnp.logical_not(owns))
+    def _():
+        for n in range(cols):
+            remote(
+                part(own, order[n]), part(mir, order[n]), mir_send.at[n, 0], mir_recv.at[order[n]], row_mate, c
+            ).wait_recv()
+
+    products(table_p, mir, run_p, 1)
+    for d in turns:
+        first = (2 * lax.rem(hi + d, half) + 1 - lo) * size
         for t in range(size):
-            y_sum[d, t] = plain_at(first + t) + y_in[d, t]
-        z_copy(d).start()
+            stage_p[d, t] = plain_at(first + t)
+        y_copy(d).start()
     for d in range(1, row_half):
         b_copy(d).wait_recv()
     total = a_sum[0]
@@ -276,6 +274,12 @@
         @pl.when(is_self(j))
         def _(j=j):
             m_in[turn] = b_sum[j * size:(j + 1) * size]
+    for d in turns[:-1]:
+        y_copy(d).wait_recv()
+        first = (2 * lax.rem(hi + d, half) + lo) * size
+        for t in range(size):
+            y_sum[d, t] = plain_at(first + t) + y_in[d, t]
+        z_copy(d).start()
     y_copy(0).wait_recv()
     for t in range(size):
         y_sum[0, t] = plain_at((2 * hi + lo) * size + t) + y_in[0, t]
@@ -334,24 +338,29 @@
 
     segment = pltpu.VMEM((cols * size, vec_count, width), vectors.dtype)
     on_vmem = pl.BlockSpec(memory_space=pltpu.VMEM)
+    in_hbm = pl.BlockSpec(memory_space=pltpu.HBM)
     return pl.pallas_call(
         functools.partial(kernel, rows, cols, width, 8 if slots % 8 == 0 else 1),
         out_shape=jax.ShapeDtypeStruct((vec_count, length), jnp.float32),
         in_specs=[
-            pl.BlockSpec(memory_space=pl.ANY),
-            pl.BlockSpec(memory_space=pl.ANY),
-            on_vmem,
-            on_vmem,
+            in_hbm,
+            in_hbm,
+            in_hbm,
+            in_hbm,
             pl.BlockSpec(memory_space=pltpu.SMEM),
         ],
         out_specs=on_vmem,
         scratch_shapes=[
             pltpu.VMEM((vec_count, length), vectors.dtype),
             pltpu.VMEM(tiles.shape, tiles.dtype),
+            pltpu.VMEM((1, slots), jnp.int32),
+            pltpu.VMEM((1, slots), jnp.int32),
             segment,
             segment,
-            pltpu.VMEM((2 * (3 + places), 1, slots), jnp.int32),
-            pltpu.SMEM((2 * (3 + places), 1, slots), jnp.int32),
+            pltpu.VMEM((3 + places, 1, slots), jnp.int32),
+            pltpu.VMEM((3 + places, 1, slots), jnp.int32),
+            pltpu.SMEM((3 + places, 1, slots), jnp.int32),
+            pltpu.SMEM((3 + places, 1, slots), jnp.int32),
             room(slots + 1),
             room(slots + 1),
             room(half, size),
@@ -364,7 +373,7 @@
             room(row_half, share * size),
             room(share * size),
             room(share, size),
-            dma((3,)), dma((half,)), dma((half,)), dma((cols,)), dma((cols, rows)), dma((cols,)),
+            dma((6,)), dma((half,)), dma((half,)), dma((cols,)), dma((cols, rows)), dma((cols,)),
             dma((half,)), dma((half,)), dma((half,)), dma((half,)),
             dma((row_half,)), dma((row_half,)), dma((row_half,)), dma((row_half,)),
             dma((share,)), dma((share,)),

time: 50.8 us -> 46.1 us (0.907); the launches traced: 49.8 us -> 45.9 us
  local copies, waits for them, and re-layouts: 4.93 us -> 1.54 us
    unnamed x9 -> x1, local copies, waits for them, and re-layouts: 4.93 us -> 1.54 us
where the time goes in v2:
time: 46.1 us; the launch traced here: 45.9 us
  Pallas kernels  43.7 us (95%)
  local copies, waits for them, and re-layouts  1.54 us (3%)
  between operations  0.66 us (1%)
    pallas_call x1, Pallas kernels, shards(): pl.pallas_call(functools.partial(kernel, rows, cols, width, 8 if slots %...  43.7 us
    unnamed x1, local copies, waits for them, and re-layouts  1.54 us

profile of v2, /device:TPU:0, one launch (start us, length us, event | category | flops | bytes accessed | tf_op | source)
XLA Modules:
  0.0 45.9 jit_solution(8741301914676641493)
XLA Ops:
  0.7 43.7 %apply_symmetric.1 = f32[16,1536]{1,0:T(8,128)} custom-call(bf16[16,1536]{1,0:T(8,128)(2,1)} %x_hbm.1, bf16[128,128,128]{2,1,0:T(8,128)(2,1)} %tiles_hbm.1, s32[1,128]{1,0:T(1,128)} %bitcast.2, s32[1,128]{1,0:T(1,128)} %bitcast.3, s32[1]{0:T(128)S(6)} %copy.7.count_ref), custom_call_target="tpu_custom_call" | custom-call | tf_op jit(solution)/shard_map/apply_symmetric/pallas_call | solution.py:342
  44.4 1.5 %copy.8 = f32[16,1536]{1,0:T(8,128)} copy(f32[16,1536]{1,0:T(8,128)} %apply_symmetric.1) | data formatting | bytes 196608
